TPU v7x, 32 devices: a whole 2x2x4 slice. The times are simulated.
32 devices in a mesh: grp: 2 (over y), seq: 4 (over z), sub: 4 (over x, core).
Axes of the slice: x: 2, y: 2, z: 4, core: 2. Of those that a mesh axis runs over, the one named last changes fastest.
Arguments:
- activations: bfloat16 [32768, 384], P(('grp', 'seq', 'sub')), parts along dimension 0, may hold values from -6 to 6
- cotangent: bfloat16 [32768, 384], P(('grp', 'seq', 'sub')), parts along dimension 0, may hold values from -6 to 6
- weights: bfloat16 [2304, 384], P('sub'), may hold values from -0.1875 to 0.1875
Outputs:
- input_grad: bfloat16 [32768, 384], P(('grp', 'seq', 'sub')), parts along dimension 0
- weight_grad: float32 [4608, 384], P(('grp', 'sub')), parts along dimension 0
There are 2 independent parts, one for each index of `grp`. A program takes and returns all parts, laid end to end along the dimension named above; an argument that names none is the same for every part. Nothing has to cross between parts.
All inputs are finite; a program needn't handle non-finite values.
Results may differ from a plain program's by a relative error of at most 0.0053.
Values may be sent and summed in bfloat16 or wider, within the bound.
A program may use at most 64 MiB of HBM per device.

v0:
```python
import math

import jax
import jax.numpy as jnp
from jax import lax
from jax.sharding import PartitionSpec as P

DILATION_FIRST = 1024
DILATION_SECOND = 2048


def from_behind(block, axis, distance):
    devices = range(lax.axis_size(axis))
    route = [(i - distance, i) for i in devices if i - distance in devices]
    return lax.ppermute(block, axis, route)


def gelu_pair(pre_act):
    coeff = 0.7978845608
    tanh_value = jnp.tanh(coeff * (pre_act + 0.044715 * pre_act * pre_act * pre_act))
    gelu_value = 0.5 * pre_act * (1.0 + tanh_value)
    gelu_slope = 0.5 * (1.0 + tanh_value) + 0.5 * pre_act * (
        1.0 - tanh_value * tanh_value
    ) * coeff * (1.0 + 3.0 * 0.044715 * pre_act * pre_act)
    return (gelu_value, gelu_slope)


def back_product(spread, kernel, count_of_rows, channels):
    spread_three = spread.reshape(count_of_rows, 3, channels)
    kernel_three = kernel.reshape(3, channels, channels)
    return lax.dot_general(
        spread_three, kernel_three, (((1, 2), (0, 2)), ((), ())), preferred_element_type=jnp.float32
    )


def tap_grads(stacked, delta):
    return lax.dot_general(
        stacked, delta, (((0,), (0,)), ((), ())), preferred_element_type=jnp.float32
    )


def per_device(activations, cotangent, weights):
    count_of_rows, channels = activations.shape
    devices = lax.axis_size("seq") * lax.axis_size("sub")
    nearby_jumps = DILATION_FIRST // count_of_rows
    distant_jumps = DILATION_SECOND // count_of_rows
    grad_scale = 1.0 / math.sqrt(count_of_rows * devices)
    all_weights = lax.all_gather(weights, "sub", axis=0, tiled=True)
    first = all_weights[: 3 * channels]
    second = all_weights[3 * channels :]

    def near_rows(source, sign):
        return from_behind(source, ("seq", "sub"), sign * nearby_jumps)

    def far_rows(source, sign):
        return from_behind(source, ("seq", "sub"), sign * distant_jumps)

    first_layer_weights = jnp.concatenate(
        (near_rows(activations, 1), activations, near_rows(activations, -1)), 1
    )
    pre_one = jnp.dot(first_layer_weights, first, preferred_element_type=jnp.float32)
    gelu_one, slope_one = gelu_pair(pre_one)
    middle_state = (activations.astype(jnp.float32) + gelu_one).astype(jnp.bfloat16)
    second_layer_weights = jnp.concatenate(
        (far_rows(middle_state, 1), middle_state, far_rows(middle_state, -1)), 1
    )
    pre_two = jnp.dot(second_layer_weights, second, preferred_element_type=jnp.float32)
    gelu_two, slope_two = gelu_pair(pre_two)
    second_error = (cotangent.astype(jnp.float32) * slope_two).astype(jnp.bfloat16)
    grad_two = tap_grads(second_layer_weights, second_error) * grad_scale
    second_reach = jnp.concatenate(
        (far_rows(second_error, -1), second_error, far_rows(second_error, 1)), 1
    )
    back_one = cotangent.astype(jnp.float32) + back_product(
        second_reach, second, count_of_rows, channels
    )
    first_error = (back_one * slope_one).astype(jnp.bfloat16)
    grad_one = tap_grads(first_layer_weights, first_error) * grad_scale
    first_reach = jnp.concatenate(
        (near_rows(first_error, -1), first_error, near_rows(first_error, 1)), 1
    )
    input_grad = (back_one + back_product(first_reach, first, count_of_rows, channels)).astype(
        jnp.bfloat16
    )
    local_grads = jnp.concatenate((grad_one, grad_two), 0)
    summed = lax.psum(local_grads, "seq")
    weight_grad = lax.psum_scatter(summed, "sub", scatter_dimension=0, tiled=True)
    return (input_grad, weight_grad)


def solution(mesh):
    placed = (P(("grp", "seq", "sub"), None), P(("grp", "seq", "sub"), None), P("sub", None))
    return jax.shard_map(
        per_device,
        mesh=mesh,
        in_specs=placed,
        out_specs=(P(("grp", "seq", "sub"), None), P(("grp", "sub"), None)),
        check_vma=False,
    )
```

profile of v0, /device:TPU:0, one launch (start us, length us, event | category | flops | bytes accessed | tf_op | source)
XLA Modules:
  0.0 237.5 jit_solution(14820011768576403430)
XLA Ops:
  7.2 0.7 all-gather.2.cloned.1.call-update
  8.0 2.4 %collective-permute-start = (bf16[1024,384]{1,0:T(8,128)(2,1)}, bf16[1024,384]{1,0:T(8,128)(2,1)S(1)}, u32[]{:S(2)}, u32[]{:S(2)}) collective-permute-start(bf16[1024,384]{1,0:T(8,128)(2,1)} %param.3), channel_id=1, source_target_pairs={{0,1},{1,2},{2,3},{3,4},{4,5},{5,6},{6,7},{7,8},{8,9},{9,10},{10,1... | collective-permute-start | bytes 2359304 | tf_op jit(solution)/shard_map/ppermute | solution.py:15
  10.4 1.3 collective-permute-start.1
  11.7 1.4 copy.6
  13.1 1.0 constant_dynamic-update-slice_fusion.2
  14.1 1.0 constant_dynamic-update-slice_fusion.1
  15.1 1.7 collective-permute-done.1
  16.8 1.0 constant_dynamic-update-slice_fusion
  17.8 22.2 %all-gather.2.cloned.1.call-done = bf16[2304,384]{1,0:T(8,128)(2,1)} async-done(((bf16[576,384]{1,0:T(8,128)(2,1)}), bf16[2304,384]{1,0:T(8,128)(2,1)}) %all-gather.2.cloned.1.call-update) | async-done | bytes 1769488 | tf_op jit(solution)/shard_map/all_gather | solution.py:48
  40.0 4.9 %add_convert_fusion = (bf16[1024,384]{0,1:T(8,128)(2,1)}, f32[1024,384]{0,1:T(8,128)}) fusion(bf16[1024,384]{0,1:T(8,128)(2,1)S(1)} %copy.6, bf16[1024,1152]{1,0:T(8,128)(2,1)} %constant_dynamic-update-slice_fusion, bf16[2304,384]{1,0:T(8,128)(2,1)} %all-gather.2.cloned.1.call-done), kind=kOutput, calls=%fused_computation.27 | convolution fusion | flops 910295040 | bytes 6389760 | tf_op jit(solution)/shard_map/dot_general | solution.py:61
  44.9 1.3 collective-permute-start.3
  46.2 7.3 %collective-permute-start.2 = (bf16[1024,384]{0,1:T(8,128)(2,1)}, bf16[1024,384]{0,1:T(8,128)(2,1)}, u32[]{:S(2)}, u32[]{:S(2)}) collective-permute-start(bf16[1024,384]{0,1:T(8,128)(2,1)} %get-tuple-element.6), channel_id=1, source_target_pairs={{0,2},{1,3},{2,4},{3,5},{4,6},{5,7},{6,8},{7,9},{8,10},{9,11},{10,... | collective-permute-start | bytes 2359304 | tf_op jit(solution)/shard_map/ppermute | solution.py:15
  53.5 0.3 copy.5
  53.8 15.1 %collective-permute-done.3 = bf16[1024,384]{0,1:T(8,128)(2,1)} collective-permute-done((bf16[1024,384]{0,1:T(8,128)(2,1)}, bf16[1024,384]{0,1:T(8,128)(2,1)}, u32[]{:S(2)}, u32[]{:S(2)}) %collective-permute-start.3) | collective-permute-done | bytes 786464 | tf_op jit(solution)/shard_map/ppermute | solution.py:15
  68.9 17.0 %collective-permute-done.2 = bf16[1024,384]{0,1:T(8,128)(2,1)} collective-permute-done((bf16[1024,384]{0,1:T(8,128)(2,1)}, bf16[1024,384]{0,1:T(8,128)(2,1)}, u32[]{:S(2)}, u32[]{:S(2)}) %collective-permute-start.2) | collective-permute-done | bytes 786464 | tf_op jit(solution)/shard_map/ppermute | solution.py:15
  85.9 3.7 %fusion = bf16[1024,384]{0,1:T(8,128)(2,1)S(1)} fusion(bf16[1024,384]{0,1:T(8,128)(2,1)S(1)} %copy.5, bf16[1024,384]{0,1:T(8,128)(2,1)} %collective-permute-done.3, bf16[1024,384]{0,1:T(8,128)(2,1)} %get-tuple-element.6, bf16[1024,384]{0,1:T(8,128)(2,1)} %collective-permute-done.2, bf16[2304,384]{1,0:T(8,128)(2,1)S(1)} %copy-done.1), kind=kOutput, calls=%fused_computation.12 | convolution fusion | flops 920911872 | bytes 4816896 | tf_op jit(solution)/shard_map/dot_general | solution.py:67
  89.6 4.4 %collective-permute-start.5 = (bf16[1024,384]{0,1:T(8,128)(2,1)S(1)}, bf16[1024,384]{0,1:T(8,128)(2,1)S(1)}, u32[]{:S(2)}, u32[]{:S(2)}) collective-permute-start(bf16[1024,384]{0,1:T(8,128)(2,1)S(1)} %fusion), channel_id=1, source_target_pairs={{0,2},{1,3},{2,4},{3,5},{4,6},{5,7},{6,8},{7,9},{8,10},{9,11},{10,... | collective-permute-start | bytes 2359304 | tf_op jit(solution)/shard_map/ppermute | solution.py:15
  94.0 1.3 collective-permute-start.4
  95.5 3.0 %convolution_multiply_fusion = f32[1152,384]{1,0:T(8,128)S(1)} fusion(bf16[1024,384]{0,1:T(8,128)(2,1)S(1)} %fusion, bf16[1024,384]{0,1:T(8,128)(2,1)} %collective-permute-done.3, bf16[1024,384]{0,1:T(8,128)(2,1)} %get-tuple-element.6, bf16[1024,384]{0,1:T(8,128)(2,1)} %collective-permute-done.2), kind=kOutput, calls=%fused_computation.1 | convolution fusion | flops 913489920 | bytes 4915200 | tf_op jit(solution)/shard_map/dot_general | solution.py:37
  98.6 29.3 %collective-permute-done.5 = bf16[1024,384]{0,1:T(8,128)(2,1)S(1)} collective-permute-done((bf16[1024,384]{0,1:T(8,128)(2,1)S(1)}, bf16[1024,384]{0,1:T(8,128)(2,1)S(1)}, u32[]{:S(2)}, u32[]{:S(2)}) %collective-permute-start.5) | collective-permute-done | bytes 786464 | tf_op jit(solution)/shard_map/ppermute | solution.py:15
  128.1 3.0 %fusion.12 = (bf16[1024,384]{0,1:T(8,128)(2,1)S(1)}, f32[1024,384]{0,1:T(8,128)}) fusion(f32[1024,384]{0,1:T(8,128)S(1)} %copy-done.4, bf16[3,384,384]{2,1,0:T(8,128)(2,1)S(1)} %bitcast.21, bf16[1024,3,384]{0,2,1:T(8,128)(2,1)S(1)} %bitcast.18, bf16[1024,384]{0,1:T(8,128)(2,1)S(1)} %copy.5), kind=kOutput, calls=%fused_computation.24 | convolution fusion | flops 914227200 | bytes 7962624 | tf_op jit(solution)/shard_map/dot_general | solution.py:31
  131.1 3.1 %convolution_multiply_fusion.1 = f32[1152,384]{1,0:T(8,128)S(1)} fusion(bf16[1024,1152]{1,0:T(8,128)(2,1)} %constant_dynamic-update-slice_fusion, bf16[1024,384]{0,1:T(8,128)(2,1)S(1)} %get-tuple-element.8), kind=kOutput, calls=%fused_computation.2 | convolution fusion | flops 906412032 | bytes 4915200 | tf_op jit(solution)/shard_map/dot_general | solution.py:37
  134.2 2.0 pad_maximum_fusion
  136.3 1.3 collective-permute-start.7
  137.6 1.3 collective-permute-start.6
  138.9 39.1 %reduce-scatter.2.cloned.1.call-done = f32[576,384]{1,0:T(8,128)} async-done(((f32[2304,384]{1,0:T(8,128)}), f32[576,384]{1,0:T(8,128)}) %reduce-scatter.2.cloned.1.call-update) | async-done | bytes 884752 | tf_op jit(solution)/shard_map/reduce_scatter | solution.py:87
  178.1 0.2 pad_maximum_fusion.3
  178.3 1.2 copy-done.3
  179.5 1.2 fusion.13
  180.7 1.2 copy.10
  181.8 47.0 %all-reduce.2.cloned.1.call-done = f32[576,384]{1,0:T(8,128)} async-done(((f32[576,384]{1,0:T(8,128)}), f32[576,384]{1,0:T(8,128)}) %all-reduce.2.cloned.1.call-update) | async-done | bytes 884752 | tf_op jit(solution)/shard_map/psum | solution.py:86
  228.8 2.1 copy.18
  (20 shorter events, 0.6 us)
Async XLA Ops:
  7.2 6.9 %copy-start = (bf16[1024,384]{1,0:T(8,128)(2,1)S(1)}, bf16[1024,384]{1,0:T(8,128)(2,1)}, u32[]{:S(2)}) copy-start(bf16[1024,384]{1,0:T(8,128)(2,1)} %param.3) | copy-start | bytes 2359300
  7.2 32.8 %all-gather.2.cloned.1.call-start = ((), (), s32[]{:S(2)}) async-start(), calls=%async_computation.1 | async-start | bytes 2211840 | tf_op jit(solution)/shard_map/all_gather | solution.py:48
  7.9 170.1 %reduce-scatter.2.cloned.1.call-start = ((), (), s32[]{:S(2)}) async-start(), calls=%async_computation.2 | async-start | bytes 4423680 | tf_op jit(solution)/shard_map/reduce_scatter | solution.py:87
  8.0 5.1 %collective-permute-start = (bf16[1024,384]{1,0:T(8,128)(2,1)}, bf16[1024,384]{1,0:T(8,128)(2,1)S(1)}, u32[]{:S(2)}, u32[]{:S(2)}) collective-permute-start(bf16[1024,384]{1,0:T(8,128)(2,1)} %param.3), channel_id=1, source_target_pairs={{0,1},{1,2},{2,3},{3,4},{4,5},{5,6},{6,7},{7,8},{8,9},{9,10},{10,1... | collective-permute-start | bytes 2359304 | tf_op jit(solution)/shard_map/ppermute | solution.py:15
  10.4 6.4 %collective-permute-start.1 = (bf16[1024,384]{1,0:T(8,128)(2,1)}, bf16[1024,384]{1,0:T(8,128)(2,1)S(1)}, u32[]{:S(2)}, u32[]{:S(2)}) collective-permute-start(bf16[1024,384]{1,0:T(8,128)(2,1)} %param.3), channel_id=1, source_target_pairs={{1,0},{2,1},{3,2},{4,3},{5,4},{6,5},{7,6},{8,7},{9,8},{10,9},{11,1... | collective-permute-start | bytes 2359304 | tf_op jit(solution)/shard_map/ppermute | solution.py:15
  17.8 35.7 %copy-start.2 = (bf16[1024,384]{1,0:T(8,128)(2,1)S(1)}, bf16[1024,384]{1,0:T(8,128)(2,1)}, u32[]{:S(2)}) copy-start(bf16[1024,384]{1,0:T(8,128)(2,1)} %param.4) | copy-start | bytes 2359300
  40.0 46.0 %copy-start.1 = (bf16[2304,384]{1,0:T(8,128)(2,1)S(1)}, bf16[2304,384]{1,0:T(8,128)(2,1)}, u32[]{:S(2)}) copy-start(bf16[2304,384]{1,0:T(8,128)(2,1)} %all-gather.2.cloned.1.call-done) | copy-start | bytes 5308420
  44.9 24.0 %collective-permute-start.3 = (bf16[1024,384]{0,1:T(8,128)(2,1)}, bf16[1024,384]{0,1:T(8,128)(2,1)}, u32[]{:S(2)}, u32[]{:S(2)}) collective-permute-start(bf16[1024,384]{0,1:T(8,128)(2,1)} %get-tuple-element.6), channel_id=1, source_target_pairs={{2,0},{3,1},{4,2},{5,3},{6,4},{7,5},{8,6},{9,7},{10,8},{11,9},{12,... | collective-permute-start | bytes 2359304 | tf_op jit(solution)/shard_map/ppermute | solution.py:15
  46.2 39.7 %collective-permute-start.2 = (bf16[1024,384]{0,1:T(8,128)(2,1)}, bf16[1024,384]{0,1:T(8,128)(2,1)}, u32[]{:S(2)}, u32[]{:S(2)}) collective-permute-start(bf16[1024,384]{0,1:T(8,128)(2,1)} %get-tuple-element.6), channel_id=1, source_target_pairs={{0,2},{1,3},{2,4},{3,5},{4,6},{5,7},{6,8},{7,9},{8,10},{9,11},{10,... | collective-permute-start | bytes 2359304 | tf_op jit(solution)/shard_map/ppermute | solution.py:15
  89.6 38.2 %collective-permute-start.5 = (bf16[1024,384]{0,1:T(8,128)(2,1)S(1)}, bf16[1024,384]{0,1:T(8,128)(2,1)S(1)}, u32[]{:S(2)}, u32[]{:S(2)}) collective-permute-start(bf16[1024,384]{0,1:T(8,128)(2,1)S(1)} %fusion), channel_id=1, source_target_pairs={{0,2},{1,3},{2,4},{3,5},{4,6},{5,7},{6,8},{7,9},{8,10},{9,11},{10,... | collective-permute-start | bytes 2359304 | tf_op jit(solution)/shard_map/ppermute | solution.py:15
  94.0 33.8 %collective-permute-start.4 = (bf16[1024,384]{0,1:T(8,128)(2,1)S(1)}, bf16[1024,384]{0,1:T(8,128)(2,1)S(1)}, u32[]{:S(2)}, u32[]{:S(2)}) collective-permute-start(bf16[1024,384]{0,1:T(8,128)(2,1)S(1)} %fusion), channel_id=1, source_target_pairs={{2,0},{3,1},{4,2},{5,3},{6,4},{7,5},{8,6},{9,7},{10,8},{11,9},{12,... | collective-permute-start | bytes 2359304 | tf_op jit(solution)/shard_map/ppermute | solution.py:15
  98.6 29.5 %copy-start.4 = (f32[1024,384]{0,1:T(8,128)S(1)}, f32[1024,384]{0,1:T(8,128)}, u32[]{:S(2)}) copy-start(f32[1024,384]{0,1:T(8,128)} %get-tuple-element.7) | copy-start | bytes 4718596
  136.2 92.6 %all-reduce.2.cloned.1.call-start = ((), (), s32[]{:S(2)}) async-start(), calls=%async_computation.3 | async-start | bytes 1769472 | tf_op jit(solution)/shard_map/psum | solution.py:86
  136.3 41.8 %collective-permute-start.7 = (bf16[1024,384]{0,1:T(8,128)(2,1)S(1)}, bf16[1024,384]{0,1:T(8,128)(2,1)S(1)}, u32[]{:S(2)}, u32[]{:S(2)}) collective-permute-start(bf16[1024,384]{0,1:T(8,128)(2,1)S(1)} %get-tuple-element.8), channel_id=1, source_target_pairs={{0,1},{1,2},{2,3},{3,4},{4,5},{5,6},{6,7},{7,8},{8,9},{9,10},{10,1... | collective-permute-start | bytes 2359304 | tf_op jit(solution)/shard_map/ppermute | solution.py:15
  137.6 40.5 %collective-permute-start.6 = (bf16[1024,384]{0,1:T(8,128)(2,1)S(1)}, bf16[1024,384]{0,1:T(8,128)(2,1)S(1)}, u32[]{:S(2)}, u32[]{:S(2)}) collective-permute-start(bf16[1024,384]{0,1:T(8,128)(2,1)S(1)} %get-tuple-element.8), channel_id=1, source_target_pairs={{1,0},{2,1},{3,2},{4,3},{5,4},{6,5},{7,6},{8,7},{9,8},{10,9},{11,1... | collective-permute-start | bytes 2359304 | tf_op jit(solution)/shard_map/ppermute | solution.py:15
  178.1 1.4 copy-start.3
Sparse Core Ops, SparseCore 0:
  9.6 30.3 all-gather.1
  136.3 41.6 reduce-scatter.1
  180.5 48.2 all-reduce.1
where the time goes:
time: 238 us; the launch traced here: 237 us
  waiting for transfers between devices  172 us (72%)
  starting transfers between devices  20.8 us (9%)
  matrix products  18.9 us (8%)
  between operations  13.9 us (6%)
  local copies, waits for them, and re-layouts  9.33 us (4%)
  other arithmetic  2.4 us (1%)
    ppermute x8, waiting for transfers between devices, from_behind(): return lax.ppermute(block, axis, route)  63.1 us
    psum x1, waiting for transfers between devices, per_device(): summed = lax.psum(local_grads, 'seq')  47 us
    reduce_scatter x1, waiting for transfers between devices, per_device(): lax.psum_scatter(summed, 'sub', scatter_dimension=0, tiled=True)  39.1 us
    all_gather x1, waiting for transfers between devices, per_device(): all_weights = lax.all_gather(weights, 'sub', axis=0, tiled=True)  22.2 us
    ppermute x8, starting transfers between devices, from_behind(): return lax.ppermute(block, axis, route)  20.7 us
    unnamed x16, local copies, waits for them, and re-layouts  8.17 us
    dot_general x2, matrix products, tap_grads(): lax.dot_general(stacked, delta, (((0,), (0,)), ((), ())), preferred_eleme...  6.12 us
    dot_general x1, matrix products, per_device(): jnp.dot(first_layer_weights, first, preferred_element_type=jnp.float32)  4.94 us
  transfers between devices with their start and end apart: 11, of which 7 were waited for; matrix products, arithmetic and copies ran while one was open for 4% of the time, Pallas kernels for 0%

commit v1 on v0

v1 whole, which is shorter than its diff:
```python
import functools
import math

import jax
import jax.numpy as jnp
from jax import lax
from jax.experimental import pallas as pl
from jax.experimental.pallas import tpu as pltpu
from jax.sharding import PartitionSpec as P

DILATION_FIRST = 1024
DILATION_SECOND = 2048
MESH = pl.DeviceIdType.MESH
CORES = 2
CHUNKS = 2
PAD = 16


def gelu_pair(pre_act):
    coeff = 0.7978845608
    tanh_value = jnp.tanh(coeff * (pre_act + 0.044715 * pre_act * pre_act * pre_act))
    gelu_value = 0.5 * pre_act * (1.0 + tanh_value)
    gelu_slope = 0.5 * (1.0 + tanh_value) + 0.5 * pre_act * (
        1.0 - tanh_value * tanh_value
    ) * coeff * (1.0 + 3.0 * 0.044715 * pre_act * pre_act)
    return (gelu_value, gelu_slope)


def kernel(
    groups, Z, S, fused, act, cot, wts, out, wg,
    A, CT, H, D2, D1, SL, B1, OG, W, WT, G, SB, RB, PB, RP, FB, OB, ssem, rsem,
):
    n, C = act.shape
    K = 3 * C
    X = S // CORES
    m = n // S
    mp = m // CHUNKS
    rows = n // CHUNKS
    tile = min(256, rows)
    y, z, s = lax.axis_index("grp"), lax.axis_index("seq"), lax.axis_index("sub")
    x, c = s // CORES, s % CORES
    other = 1 - c
    grad_scale = 1.0 / math.sqrt(n * S * Z)
    f32, bf16 = jnp.float32, jnp.bfloat16

    slots = {}

    def copy(name, src, dst, where):
        i = slots.setdefault(name, len(slots))
        return pltpu.make_async_remote_copy(
            src_ref=src, dst_ref=dst, send_sem=ssem.at[i], recv_sem=rsem.at[i],
            device_id=where, device_id_type=MESH,
        )

    def span(start, size):
        return pl.ds(pl.multiple_of(start, 16), size)

    pending = []

    barrier = pltpu.get_barrier_semaphore()
    greeted = 0

    def greet(where):
        pl.semaphore_signal(barrier, inc=1, device_id=where, device_id_type=MESH)

    for j in range(1, S):
        greet((y, z, (s + j) % S))
        greeted += 1
    for j in range(1, Z):
        for i in range(X) if fused else range(1):
            greet((y, (z + j) % Z, ((x + i) % X) * CORES + c))
            greeted += 1
    greet((1 - y, z, s))
    greeted += 1
    pl.semaphore_wait(barrier, greeted)

    w = wts.shape[0]
    hw = w // 2
    partner = (y, z, x * CORES + other)

    def half(shard, which):
        return W.at[span((shard * 2 + which) * hw, hw)]

    W[span(s * w, w), :] = wts[...]
    for j in range(1, X):
        d = copy(("wx", j), wts.at[span(y * hw, hw)], half(s, y), (y, z, ((x + j) % X) * CORES + c))
        d.start()
        pending.append(d)
    d = copy("wc", wts, W.at[span(s * w, w)], partner)
    d.start()
    pending.append(d)

    def spread(kind, source, target, lead, p):
        found = []
        for j in range(1, S):
            to = (s + j) % S
            d = copy(
                (kind, p, j), source.at[span(to * m + p * mp, mp)],
                target.at[p, span((lead + s) * mp, mp)], (y, z, to),
            )
            d.start()
            pending.append(d)
            found.append(d)
        target[p, span((lead + s) * mp, mp), :] = source[span(s * m + p * mp, mp), :]
        return found

    acts = [spread("a", act, A, 1, p) for p in range(CHUNKS)]

    def edges(buf, width):
        size = width * mp

        @pl.when(z == 0)
        def _():
            for p in range(CHUNKS):
                buf[p, 0:size, :] = jnp.zeros((size, C), bf16)

        @pl.when(z == Z - 1)
        def _():
            for p in range(CHUNKS):
                buf[p, size + rows : 2 * size + rows, :] = jnp.zeros((size, C), bf16)

    edges(A, 1)
    edges(H, 2)
    edges(D2, 2)
    edges(D1, 1)
    if fused:
        PB[...] = jnp.zeros(PB.shape, bf16)

    halos = []

    def halo_pair(kind, buf, width, p):
        size = width * mp
        up = copy(
            (kind, "up", p), buf.at[p, pl.ds(rows, size)], buf.at[p, pl.ds(0, size)],
            (y, jnp.minimum(z + 1, Z - 1), s),
        )
        down = copy(
            (kind, "down", p), buf.at[p, pl.ds(size, size)], buf.at[p, pl.ds(size + rows, size)],
            (y, jnp.maximum(z - 1, 0), s),
        )
        return up, down

    def halo_send(kind, buf, width, p):
        up, down = halo_pair(kind, buf, width, p)

        @pl.when(z < Z - 1)
        def _():
            up.start()

        @pl.when(z > 0)
        def _():
            down.start()

        halos.append((kind, buf, width, p))

    def halo_wait(kind, buf, width, p):
        up, down = halo_pair(kind, buf, width, p)

        @pl.when(z > 0)
        def _():
            up.wait_recv()

        @pl.when(z < Z - 1)
        def _():
            down.wait_recv()

    forwards = []
    for j in range(1, X):
        source = ((x + X - j) % X) * CORES + c
        copy(("wx", j), half(source, y), half(source, y), partner).wait_recv()
        d = copy(("wy", j), half(source, y), half(source, y), (1 - y, z, s))
        d.start()
        pending.append(d)
        d = copy(("wca", j), half(source, y), half(source, y), partner)
        d.start()
        pending.append(d)
    for j in range(1, X):
        source = ((x + X - j) % X) * CORES + c
        theirs = half(source, 1 - y)
        copy(("wy", j), theirs, theirs, partner).wait_recv()
        d = copy(("wcb", j), theirs, theirs, partner)
        d.start()
        pending.append(d)

    for p in range(CHUNKS):
        for d in acts[p]:
            d.wait_recv()
        halo_send("ha", A, 1, p)
    cots = [spread("c", cot, CT, 0, p) for p in range(CHUNKS)]

    pending[X - 1].wait_recv()
    for j in range(1, X):
        source = ((x + X - j) % X) * CORES + other
        copy(("wca", j), half(source, y), half(source, y), partner).wait_recv()
        copy(("wcb", j), half(source, 1 - y), half(source, 1 - y), partner).wait_recv()
    for k in range(6):
        WT[k * C : (k + 1) * C, :] = W[k * C : (k + 1) * C, :].T

    def three(buf, p, width, start, back):
        taps = [buf[p, span(start + k * width * mp, tile), :] for k in range(3)]
        return jnp.concatenate(taps[::-1] if back else taps, 1)

    def tiles(body):
        def step(t, carry):
            body(t * tile)
            return carry

        lax.fori_loop(0, rows // tile, step, 0)

    for p in range(CHUNKS):
        halo_wait("ha", A, 1, p)

        def layer_one(start):
            pre = jnp.dot(three(A, p, 1, start, False), W[0:K, :], preferred_element_type=f32)
            value, slope = gelu_pair(pre)
            SL[p, span(start, tile), :] = slope
            own = A[p, span(start + mp, tile), :].astype(f32)
            H[p, span(start + 2 * mp, tile), :] = (own + value).astype(bf16)

        tiles(layer_one)
        halo_send("hh", H, 2, p)

    for p in range(CHUNKS):
        for d in cots[p]:
            d.wait_recv()
        halo_wait("hh", H, 2, p)

        def layer_two(start):
            pre = jnp.dot(three(H, p, 2, start, False), W[K : 2 * K, :], preferred_element_type=f32)
            slope = gelu_pair(pre)[1]
            here = CT[p, span(start, tile), :].astype(f32)
            D2[p, span(start + 2 * mp, tile), :] = (here * slope).astype(bf16)

        tiles(layer_two)
        halo_send("hd", D2, 2, p)

    def grads(layer, buf, width, delta):
        for k in range(3):
            total = None
            for p in range(CHUNKS):
                part = lax.dot_general(
                    buf[p, k * width * mp : k * width * mp + rows, :],
                    delta[p, width * mp : width * mp + rows, :],
                    (((0,), (0,)), ((), ())), preferred_element_type=f32,
                )
                total = part if total is None else total + part
            G[layer, k * C : (k + 1) * C, :] = total

    hk = K // 2
    ring = Z * X
    me = z * X + x
    piece = hk // ring

    def pair_send(layer):
        SB[layer, :, :] = G[layer, span(other * hk, hk), :].astype(bf16)
        d = copy(("pair", layer), SB.at[layer], RB.at[layer], partner)
        d.start()
        pending.append(d)
        return d

    def scatter(layer, d):
        d.wait_recv()
        found = []
        for k in range(ring):
            mine = G[layer, pl.ds(pl.multiple_of(c * hk + k * piece, 8), piece), :]
            PB[layer, k, 0:piece, :] = (
                mine + RB[layer, k * piece : (k + 1) * piece, :].astype(f32)
            ).astype(bf16)
        for j in range(1, ring):
            to = (me + j) % ring
            d = copy(
                ("rs", layer, j), PB.at[layer, to], RP.at[layer, j - 1],
                (y, to // X, (to % X) * CORES + c),
            )
            d.start()
            pending.append(d)
            found.append(d)
        return found

    gathers = []

    def gather_copy(layer, xs, dz):
        return copy(
            ("ag", xs, dz), FB.at[layer], OB.at[me], (y, (z + dz) % Z, layer * CORES + c)
        )

    def gather(layer, found):
        total = PB[layer, me].astype(f32)
        for j, d in enumerate(found):
            d.wait_recv()
            total = total + RP[layer, j].astype(f32)
        FB[layer] = (total * grad_scale).astype(bf16)
        for xs in range(X):

            @pl.when(x == xs)
            def _():
                for dz in range(Z):
                    if xs == layer and dz == 0:
                        OB[me] = FB[layer]
                    else:
                        gather_copy(layer, xs, dz).start()

            gathers.append((layer, xs))

    grads(1, H, 2, D2)
    if fused:
        pair_two = pair_send(1)

    for p in range(CHUNKS):
        halo_wait("hd", D2, 2, p)

        def back_two(start):
            total = CT[p, span(start, tile), :].astype(f32) + jnp.dot(
                three(D2, p, 2, start, True), WT[K : 2 * K, :], preferred_element_type=f32
            )
            B1[p, span(start, tile), :] = total
            D1[p, span(start + mp, tile), :] = (total * SL[p, span(start, tile), :]).astype(bf16)

        tiles(back_two)
        halo_send("he", D1, 1, p)

    if fused:
        found_two = scatter(1, pair_two)
    grads(0, A, 1, D1)
    if fused:
        pair_one = pair_send(0)

    for p in range(CHUNKS):
        halo_wait("he", D1, 1, p)

        def back_one(start):
            OG[p, span(start, tile), :] = (
                B1[p, span(start, tile), :]
                + jnp.dot(three(D1, p, 1, start, True), WT[0:K, :], preferred_element_type=f32)
            ).astype(bf16)

        tiles(back_one)
        if fused and p == 0:
            found_one = scatter(0, pair_one)
        for j in range(1, S):
            to = (s + j) % S
            d = copy(
                ("o", p, j), OG.at[p, span(to * mp, mp)], out.at[span(s * m + p * mp, mp)],
                (y, z, to),
            )
            d.start()
            pending.append(d)
        out[span(s * m + p * mp, mp), :] = OG[p, span(s * mp, mp), :]

    if fused:
        gather(1, found_two)
        gather(0, found_one)
        for layer in range(2):

            @pl.when(x == layer)
            def _():
                for xs in range(X):
                    for dz in range(Z):
                        if xs != layer or dz != 0:
                            gather_copy(layer, xs, dz).wait_recv()
                for k in range(ring):
                    wg[k * piece : (k + 1) * piece, :] = OB[k, 0:piece, :].astype(f32)
    else:
        wg[...] = G[...].reshape(2 * K, C)

    for p in range(CHUNKS):
        for j in range(1, S):
            came = out.at[span(((s + S - j) % S) * m + p * mp, mp)]
            copy(("o", p, j), came, came, partner).wait_recv()
    for d in pending:
        d.wait_send()
    for kind, buf, width, p in halos:
        up, down = halo_pair(kind, buf, width, p)
        pl.when(z < Z - 1)(up.wait_send)
        pl.when(z > 0)(down.wait_send)
    for layer, xs in gathers:

        @pl.when(x == xs)
        def _():
            for dz in range(Z):
                if xs != layer or dz != 0:
                    gather_copy(layer, xs, dz).wait_send()


def per_device(groups, Z, S, activations, cotangent, weights):
    n, C = activations.shape
    assert n == DILATION_FIRST and 2 * n == DILATION_SECOND and groups == 2 and S >= 2 * CORES
    K = 3 * C
    X = S // CORES
    ring = Z * X
    mp = n // S // CHUNKS
    rows = n // CHUNKS
    fused = X == 2 and (K // 2) % (8 * ring) == 0
    piece = K // 2 // ring if fused else PAD
    padded = -(-piece // PAD) * PAD
    pieces = ring if fused else 2
    hk = K // 2 if fused else PAD
    bf16, f32 = jnp.bfloat16, jnp.float32
    semaphores = (S - 1) * CHUNKS * 3 + 8 * CHUNKS + 1 + 4 * X + 2 * (1 + ring) + ring + 8
    vmem = pl.BlockSpec(memory_space=pltpu.VMEM)
    input_grad, grads = pl.pallas_call(
        functools.partial(kernel, groups, Z, S, fused),
        out_shape=(
            jax.ShapeDtypeStruct((n, C), bf16),
            jax.ShapeDtypeStruct((weights.shape[0] if fused else 2 * K, C), f32),
        ),
        in_specs=[vmem] * 3,
        out_specs=(vmem, vmem),
        scratch_shapes=[
            pltpu.VMEM((CHUNKS, rows + 2 * mp, C), bf16),
            pltpu.VMEM((CHUNKS, rows, C), bf16),
            pltpu.VMEM((CHUNKS, rows + 4 * mp, C), bf16),
            pltpu.VMEM((CHUNKS, rows + 4 * mp, C), bf16),
            pltpu.VMEM((CHUNKS, rows + 2 * mp, C), bf16),
            pltpu.VMEM((CHUNKS, rows, C), f32),
            pltpu.VMEM((CHUNKS, rows, C), f32),
            pltpu.VMEM((CHUNKS, rows, C), bf16),
            pltpu.VMEM((2 * K, C), bf16),
            pltpu.VMEM((2 * K, C), bf16),
            pltpu.VMEM((2, K, C), f32),
            pltpu.VMEM((2, hk, C), bf16),
            pltpu.VMEM((2, hk, C), bf16),
            pltpu.VMEM((2, pieces, padded, C), bf16),
            pltpu.VMEM((2, pieces - 1, padded, C), bf16),
            pltpu.VMEM((2, padded, C), bf16),
            pltpu.VMEM((pieces, padded, C), bf16),
            pltpu.SemaphoreType.DMA((semaphores,)),
            pltpu.SemaphoreType.DMA((semaphores,)),
        ],
        compiler_params=pltpu.CompilerParams(
            collective_id=0, has_side_effects=True, vmem_limit_bytes=48 * 1024 * 1024
        ),
        name="layers_backward",
    )(activations, cotangent, weights)
    if not fused:
        scale = 1.0 / math.sqrt(n * S * Z)
        grads = lax.psum(grads * scale, "seq")
        grads = lax.psum_scatter(grads, "sub", scatter_dimension=0, tiled=True)
    return (input_grad, grads)


def solution(mesh):
    placed = (P(("grp", "seq", "sub"), None), P(("grp", "seq", "sub"), None), P("sub", None))
    sizes = [mesh.shape[axis] for axis in ("grp", "seq", "sub")]
    return jax.shard_map(
        functools.partial(per_device, *sizes),
        mesh=mesh,
        in_specs=placed,
        out_specs=(P(("grp", "seq", "sub"), None), P(("grp", "sub"), None)),
        check_vma=False,
    )
```

time: 238 us -> 87 us (0.37)
  waiting for transfers between devices: 172 us -> 0 us
  Pallas kernels: 0 us -> 81 us
  starting transfers between devices: 20.8 us -> 0 us
  matrix products: 18.9 us -> 0 us
  between operations: 13.9 us -> 0.65 us
  local copies, waits for them, and re-layouts: 9.33 us -> 5.06 us
  other arithmetic: 2.4 us -> 0 us
    pallas_call x0 -> x1, Pallas kernels: none -> 81 us  [per_device(): pl.pallas_call(functools.partial(kernel, groups, Z, S, fused), out_shape=...]
    ppermute x8 -> x0, waiting for transfers between devices: 63.1 us -> none  [from_behind(): return lax.ppermute(block, axis, route)]
    psum x1 -> x0, waiting for transfers between devices: 47 us -> none  [per_device(): summed = lax.psum(local_grads, 'seq')]
    reduce_scatter x1 -> x0, waiting for transfers between devices: 39.1 us -> none  [per_device(): lax.psum_scatter(summed, 'sub', scatter_dimension=0, tiled=True)]
    all_gather x1 -> x0, waiting for transfers between devices: 22.2 us -> none  [per_device(): all_weights = lax.all_gather(weights, 'sub', axis=0, tiled=True)]
    ppermute x8 -> x0, starting transfers between devices: 20.7 us -> none  [from_behind(): return lax.ppermute(block, axis, route)]
    dot_general x6 -> x0, matrix products: 18.9 us -> none  [the longest x2 6.12 us: tap_grads(): lax.dot_general(stacked, delta, (((0,), (0,)), ((), ())), preferred_eleme...]
    unnamed x16 -> x8, local copies, waits for them, and re-layouts: 8.17 us -> 5.06 us
  transfers between devices with their start and end apart: 11 -> 0, of which waited for: 7 -> 0; matrix products, arithmetic and copies ran while one was open for 4% -> 0% of each run, Pallas kernels for 0% -> 0%
where the time goes in v1:
time: 87 us; the launch traced here: 86.7 us
  Pallas kernels  81 us (93%)
  local copies, waits for them, and re-layouts  5.06 us (6%)
    pallas_call x1, Pallas kernels, per_device(): pl.pallas_call(functools.partial(kernel, groups, Z, S, fused), out_shape=...  81 us
    unnamed x8, local copies, waits for them, and re-layouts  5.06 us

profile of v1, /device:TPU:0, one launch (start us, length us, event | category | flops | bytes accessed | tf_op | source)
XLA Modules:
  0.0 86.7 jit_solution(8576049059421867335)
XLA Ops:
  0.6 0.0 copy-start
  0.6 1.1 %copy-done = bf16[1024,384]{1,0:T(8,128)(2,1)S(1)} copy-done((bf16[1024,384]{1,0:T(8,128)(2,1)S(1)}, bf16[1024,384]{1,0:T(8,128)(2,1)}, u32[]{:S(2)}) %copy-start) | copy-done | bytes 786456
  1.8 0.0 copy-start.1
  1.8 1.1 %copy-done.1 = bf16[1024,384]{1,0:T(8,128)(2,1)S(1)} copy-done((bf16[1024,384]{1,0:T(8,128)(2,1)S(1)}, bf16[1024,384]{1,0:T(8,128)(2,1)}, u32[]{:S(2)}) %copy-start.1) | copy-done | bytes 786456
  2.9 0.0 copy-start.2
  2.9 1.0 %copy-done.2 = bf16[576,384]{1,0:T(8,128)(2,1)S(1)} copy-done((bf16[576,384]{1,0:T(8,128)(2,1)S(1)}, bf16[576,384]{1,0:T(8,128)(2,1)}, u32[]{:S(2)}) %copy-start.2) | copy-done | bytes 442392
  3.9 81.0 %layers_backward.1 = (bf16[1024,384]{1,0:T(8,128)(2,1)S(1)}, f32[576,384]{1,0:T(8,128)S(1)}) custom-call(bf16[1024,384]{1,0:T(8,128)(2,1)S(1)} %copy-done, bf16[1024,384]{1,0:T(8,128)(2,1)S(1)} %copy-done.1, bf16[576,384]{1,0:T(8,128)(2,1)S(1)} %copy-done.2), custom_call_target="tpu_custom_call" | custom-call | tf_op jit(solution)/shard_map/layers_backward/pallas_call | solution.py:401
  84.9 0.9 %copy.7 = bf16[1024,384]{1,0:T(8,128)(2,1)} copy(bf16[1024,384]{1,0:T(8,128)(2,1)S(1)} %get-tuple-element.4) | data formatting | bytes 1572864
  85.8 0.9 %copy.8 = f32[576,384]{1,0:T(8,128)} copy(f32[576,384]{1,0:T(8,128)S(1)} %get-tuple-element.5) | data formatting | bytes 1769472
Async XLA Ops:
  0.6 1.1 %copy-start = (bf16[1024,384]{1,0:T(8,128)(2,1)S(1)}, bf16[1024,384]{1,0:T(8,128)(2,1)}, u32[]{:S(2)}) copy-start(bf16[1024,384]{1,0:T(8,128)(2,1)} %act.1) | copy-start | bytes 2359300
  1.8 1.1 %copy-start.1 = (bf16[1024,384]{1,0:T(8,128)(2,1)S(1)}, bf16[1024,384]{1,0:T(8,128)(2,1)}, u32[]{:S(2)}) copy-start(bf16[1024,384]{1,0:T(8,128)(2,1)} %cot.1) | copy-start | bytes 2359300
  2.9 1.0 %copy-start.2 = (bf16[576,384]{1,0:T(8,128)(2,1)S(1)}, bf16[576,384]{1,0:T(8,128)(2,1)}, u32[]{:S(2)}) copy-start(bf16[576,384]{1,0:T(8,128)(2,1)} %wts.1) | copy-start | bytes 1327108

commit v2 on v1

--- a/solution.py
+++ b/solution.py
@@ -28,7 +28,7 @@
 
 def kernel(
     groups, Z, S, fused, act, cot, wts, out, wg,
-    A, CT, H, D2, D1, SL, B1, OG, W, WT, G, SB, RB, PB, RP, FB, OB, ssem, rsem,
+    A, CT, H, D2, D1, SL, B1, OG, W, WT, G, SB, RB, XB, XR, PB, RP, FB, OB, ssem, rsem, lsem,
 ):
     n, C = act.shape
     K = 3 * C
@@ -56,6 +56,11 @@
         return pl.ds(pl.multiple_of(start, 16), size)
 
     pending = []
+    local = {}
+
+    def bring(name, src, dst):
+        local[name] = pltpu.make_async_copy(src, dst, lsem.at[len(local)])
+        local[name].start()
 
     barrier = pltpu.get_barrier_semaphore()
     greeted = 0
@@ -67,9 +72,8 @@
         greet((y, z, (s + j) % S))
         greeted += 1
     for j in range(1, Z):
-        for i in range(X) if fused else range(1):
-            greet((y, (z + j) % Z, ((x + i) % X) * CORES + c))
-            greeted += 1
+        greet((y, (z + j) % Z, s))
+        greeted += 1
     greet((1 - y, z, s))
     greeted += 1
     pl.semaphore_wait(barrier, greeted)
@@ -81,7 +85,6 @@
     def half(shard, which):
         return W.at[span((shard * 2 + which) * hw, hw)]
 
-    W[span(s * w, w), :] = wts[...]
     for j in range(1, X):
         d = copy(("wx", j), wts.at[span(y * hw, hw)], half(s, y), (y, z, ((x + j) % X) * CORES + c))
         d.start()
@@ -101,10 +104,14 @@
             d.start()
             pending.append(d)
             found.append(d)
-        target[p, span((lead + s) * mp, mp), :] = source[span(s * m + p * mp, mp), :]
+        bring(
+            (kind, p), source.at[span(s * m + p * mp, mp)],
+            target.at[p, span((lead + s) * mp, mp)],
+        )
         return found
 
     acts = [spread("a", act, A, 1, p) for p in range(CHUNKS)]
+    bring("w", wts, W.at[span(s * w, w)])
 
     def edges(buf, width):
         size = width * mp
@@ -183,18 +190,18 @@
         pending.append(d)
 
     for p in range(CHUNKS):
+        local["a", p].wait()
         for d in acts[p]:
             d.wait_recv()
         halo_send("ha", A, 1, p)
     cots = [spread("c", cot, CT, 0, p) for p in range(CHUNKS)]
 
+    local["w"].wait()
     pending[X - 1].wait_recv()
     for j in range(1, X):
         source = ((x + X - j) % X) * CORES + other
         copy(("wca", j), half(source, y), half(source, y), partner).wait_recv()
         copy(("wcb", j), half(source, 1 - y), half(source, 1 - y), partner).wait_recv()
-    for k in range(6):
-        WT[k * C : (k + 1) * C, :] = W[k * C : (k + 1) * C, :].T
 
     def three(buf, p, width, start, back):
         taps = [buf[p, span(start + k * width * mp, tile), :] for k in range(3)]
@@ -220,7 +227,11 @@
         tiles(layer_one)
         halo_send("hh", H, 2, p)
 
-    for p in range(CHUNKS):
+    for k in range(6):
+        WT[k * C : (k + 1) * C, :] = W[k * C : (k + 1) * C, :].T
+
+    for p in range(CHUNKS):
+        local["c", p].wait()
         for d in cots[p]:
             d.wait_recv()
         halo_wait("hh", H, 2, p)
@@ -247,9 +258,8 @@
             G[layer, k * C : (k + 1) * C, :] = total
 
     hk = K // 2
-    ring = Z * X
-    me = z * X + x
-    piece = hk // ring
+    qk = hk // 2
+    piece = qk // Z
 
     def pair_send(layer):
         SB[layer, :, :] = G[layer, span(other * hk, hk), :].astype(bf16)
@@ -258,49 +268,81 @@
         pending.append(d)
         return d
 
+    def across_x(layer, d):
+        d.wait_recv()
+        there = (1 - x) * qk
+        XB[layer] = (
+            G[layer, span(c * hk + there, qk), :] + RB[layer, span(there, qk), :].astype(f32)
+        ).astype(bf16)
+        d = copy(("x", layer), XB.at[layer], XR.at[layer], (y, z, (1 - x) * CORES + c))
+        d.start()
+        pending.append(d)
+        return d
+
     def scatter(layer, d):
+        here = x * qk
+        both = G[layer, span(c * hk + here, qk), :] + RB[layer, span(here, qk), :].astype(f32)
         d.wait_recv()
+        both = (both + XR[layer].astype(f32)).astype(bf16)
+        for k in range(Z):
+            PB[layer, k, 0:piece, :] = both[k * piece : (k + 1) * piece, :]
         found = []
-        for k in range(ring):
-            mine = G[layer, pl.ds(pl.multiple_of(c * hk + k * piece, 8), piece), :]
-            PB[layer, k, 0:piece, :] = (
-                mine + RB[layer, k * piece : (k + 1) * piece, :].astype(f32)
-            ).astype(bf16)
-        for j in range(1, ring):
-            to = (me + j) % ring
-            d = copy(
-                ("rs", layer, j), PB.at[layer, to], RP.at[layer, j - 1],
-                (y, to // X, (to % X) * CORES + c),
-            )
+        for j in range(1, Z):
+            to = (z + j) % Z
+            d = copy(("rs", layer, j), PB.at[layer, to], RP.at[layer, j - 1], (y, to, s))
             d.start()
             pending.append(d)
             found.append(d)
         return found
 
-    gathers = []
-
-    def gather_copy(layer, xs, dz):
-        return copy(
-            ("ag", xs, dz), FB.at[layer], OB.at[me], (y, (z + dz) % Z, layer * CORES + c)
-        )
+    def give(layer):
+        at = OB.at[1 - layer, z]
+        return copy("give", FB.at[layer], at, (y, z, layer * CORES + c))
+
+    def along_z(which, dz):
+        at = OB.at[which, z]
+        return copy(("ag", which, dz), at, at, (y, (z + dz) % Z, s))
 
     def gather(layer, found):
-        total = PB[layer, me].astype(f32)
+        total = PB[layer, z].astype(f32)
         for j, d in enumerate(found):
             d.wait_recv()
             total = total + RP[layer, j].astype(f32)
-        FB[layer] = (total * grad_scale).astype(bf16)
-        for xs in range(X):
-
-            @pl.when(x == xs)
-            def _():
-                for dz in range(Z):
-                    if xs == layer and dz == 0:
-                        OB[me] = FB[layer]
-                    else:
-                        gather_copy(layer, xs, dz).start()
-
-            gathers.append((layer, xs))
+        result = (total * grad_scale).astype(bf16)
+
+        @pl.when(x == layer)
+        def _():
+            OB[layer, z] = result
+            for dz in range(1, Z):
+                along_z(layer, dz).start()
+
+        @pl.when(x != layer)
+        def _():
+            FB[layer] = result
+            give(layer).start()
+
+    def pass_on(layer):
+        @pl.when(x == layer)
+        def _():
+            give(layer).wait_recv()
+            for dz in range(1, Z):
+                along_z(1 - layer, dz).start()
+
+    def collect(layer):
+        @pl.when(x == layer)
+        def _():
+            for which in range(2):
+                for dz in range(1, Z):
+                    along_z(which, dz).wait_recv()
+            for which in range(2):
+                for k in range(Z):
+                    row = which * qk + k * piece
+                    wg[row : row + piece, :] = OB[which, k, 0:piece, :].astype(f32)
+            for which in range(2):
+                for dz in range(1, Z):
+                    along_z(which, dz).wait_send()
+
+        pl.when(x != layer)(give(layer).wait_send)
 
     grads(1, H, 2, D2)
     if fused:
@@ -320,10 +362,12 @@
         halo_send("he", D1, 1, p)
 
     if fused:
-        found_two = scatter(1, pair_two)
+        cross_two = across_x(1, pair_two)
     grads(0, A, 1, D1)
     if fused:
         pair_one = pair_send(0)
+        found_two = scatter(1, cross_two)
+        cross_one = across_x(0, pair_one)
 
     for p in range(CHUNKS):
         halo_wait("he", D1, 1, p)
@@ -336,7 +380,7 @@
 
         tiles(back_one)
         if fused and p == 0:
-            found_one = scatter(0, pair_one)
+            found_one = scatter(0, cross_one)
         for j in range(1, S):
             to = (s + j) % S
             d = copy(
@@ -350,16 +394,10 @@
     if fused:
         gather(1, found_two)
         gather(0, found_one)
-        for layer in range(2):
-
-            @pl.when(x == layer)
-            def _():
-                for xs in range(X):
-                    for dz in range(Z):
-                        if xs != layer or dz != 0:
-                            gather_copy(layer, xs, dz).wait_recv()
-                for k in range(ring):
-                    wg[k * piece : (k + 1) * piece, :] = OB[k, 0:piece, :].astype(f32)
+        pass_on(1)
+        pass_on(0)
+        collect(1)
+        collect(0)
     else:
         wg[...] = G[...].reshape(2 * K, C)
 
@@ -373,13 +411,6 @@
         up, down = halo_pair(kind, buf, width, p)
         pl.when(z < Z - 1)(up.wait_send)
         pl.when(z > 0)(down.wait_send)
-    for layer, xs in gathers:
-
-        @pl.when(x == xs)
-        def _():
-            for dz in range(Z):
-                if xs != layer or dz != 0:
-                    gather_copy(layer, xs, dz).wait_send()
 
 
 def per_device(groups, Z, S, activations, cotangent, weights):
@@ -387,16 +418,16 @@
     assert n == DILATION_FIRST and 2 * n == DILATION_SECOND and groups == 2 and S >= 2 * CORES
     K = 3 * C
     X = S // CORES
-    ring = Z * X
     mp = n // S // CHUNKS
     rows = n // CHUNKS
-    fused = X == 2 and (K // 2) % (8 * ring) == 0
-    piece = K // 2 // ring if fused else PAD
+    fused = X == 2 and (K // 4) % (8 * Z) == 0 and (K // 4) % PAD == 0
+    piece = K // 4 // Z if fused else PAD
     padded = -(-piece // PAD) * PAD
-    pieces = ring if fused else 2
+    pieces = Z if fused else 2
+    qk = K // 4 if fused else PAD
     hk = K // 2 if fused else PAD
     bf16, f32 = jnp.bfloat16, jnp.float32
-    semaphores = (S - 1) * CHUNKS * 3 + 8 * CHUNKS + 1 + 4 * X + 2 * (1 + ring) + ring + 8
+    semaphores = (S - 1) * CHUNKS * 3 + 8 * CHUNKS + 1 + 4 * X + 2 * (2 + Z) + 1 + 2 * Z + 8
     vmem = pl.BlockSpec(memory_space=pltpu.VMEM)
     input_grad, grads = pl.pallas_call(
         functools.partial(kernel, groups, Z, S, fused),
@@ -404,7 +435,7 @@
             jax.ShapeDtypeStruct((n, C), bf16),
             jax.ShapeDtypeStruct((weights.shape[0] if fused else 2 * K, C), f32),
         ),
-        in_specs=[vmem] * 3,
+        in_specs=[pl.BlockSpec(memory_space=pltpu.HBM)] * 3,
         out_specs=(vmem, vmem),
         scratch_shapes=[
             pltpu.VMEM((CHUNKS, rows + 2 * mp, C), bf16),
@@ -420,12 +451,15 @@
             pltpu.VMEM((2, K, C), f32),
             pltpu.VMEM((2, hk, C), bf16),
             pltpu.VMEM((2, hk, C), bf16),
+            pltpu.VMEM((2, qk, C), bf16),
+            pltpu.VMEM((2, qk, C), bf16),
             pltpu.VMEM((2, pieces, padded, C), bf16),
             pltpu.VMEM((2, pieces - 1, padded, C), bf16),
             pltpu.VMEM((2, padded, C), bf16),
-            pltpu.VMEM((pieces, padded, C), bf16),
+            pltpu.VMEM((2, pieces, padded, C), bf16),
             pltpu.SemaphoreType.DMA((semaphores,)),
             pltpu.SemaphoreType.DMA((semaphores,)),
+            pltpu.SemaphoreType.DMA((2 * CHUNKS + 1,)),
         ],
         compiler_params=pltpu.CompilerParams(
             collective_id=0, has_side_effects=True, vmem_limit_bytes=48 * 1024 * 1024

time: 87 us -> 77.7 us (0.89)
  Pallas kernels: 81 us -> 71.7 us
    pallas_call x1, Pallas kernels: 81 us -> 71.7 us  [per_device(): pl.pallas_call(functools.partial(kernel, groups, Z, S, fused), out_shape=...]
where the time goes in v2:
time: 77.7 us; the launch traced here: 77.4 us
  Pallas kernels  71.7 us (92%)
  local copies, waits for them, and re-layouts  5.06 us (7%)
    pallas_call x1, Pallas kernels, per_device(): pl.pallas_call(functools.partial(kernel, groups, Z, S, fused), out_shape=...  71.7 us
    unnamed x8, local copies, waits for them, and re-layouts  5.06 us

profile of v2, /device:TPU:0, one launch (start us, length us, event | category | flops | bytes accessed | tf_op | source)
XLA Modules:
  0.0 77.4 jit_solution(11457007804682697848)
XLA Ops:
  0.6 0.0 copy-start
  0.6 1.1 %copy-done = bf16[1024,384]{1,0:T(8,128)(2,1)S(1)} copy-done((bf16[1024,384]{1,0:T(8,128)(2,1)S(1)}, bf16[1024,384]{1,0:T(8,128)(2,1)}, u32[]{:S(2)}) %copy-start) | copy-done | bytes 786456
  1.8 0.0 copy-start.1
  1.8 1.1 %copy-done.1 = bf16[1024,384]{1,0:T(8,128)(2,1)S(1)} copy-done((bf16[1024,384]{1,0:T(8,128)(2,1)S(1)}, bf16[1024,384]{1,0:T(8,128)(2,1)}, u32[]{:S(2)}) %copy-start.1) | copy-done | bytes 786456
  2.9 0.0 copy-start.2
  2.9 1.0 %copy-done.2 = bf16[576,384]{1,0:T(8,128)(2,1)S(1)} copy-done((bf16[576,384]{1,0:T(8,128)(2,1)S(1)}, bf16[576,384]{1,0:T(8,128)(2,1)}, u32[]{:S(2)}) %copy-start.2) | copy-done | bytes 442392
  3.9 71.7 %layers_backward.1 = (bf16[1024,384]{1,0:T(8,128)(2,1)S(1)}, f32[576,384]{1,0:T(8,128)S(1)}) custom-call(bf16[1024,384]{1,0:T(8,128)(2,1)S(1)} %copy-done, bf16[1024,384]{1,0:T(8,128)(2,1)S(1)} %copy-done.1, bf16[576,384]{1,0:T(8,128)(2,1)S(1)} %copy-done.2), custom_call_target="tpu_custom_call" | custom-call | tf_op jit(solution)/shard_map/layers_backward/pallas_call | solution.py:432
  75.6 0.9 %copy.7 = bf16[1024,384]{1,0:T(8,128)(2,1)} copy(bf16[1024,384]{1,0:T(8,128)(2,1)S(1)} %get-tuple-element.4) | data formatting | bytes 1572864
  76.5 0.9 %copy.8 = f32[576,384]{1,0:T(8,128)} copy(f32[576,384]{1,0:T(8,128)S(1)} %get-tuple-element.5) | data formatting | bytes 1769472
Async XLA Ops:
  0.6 1.1 %copy-start = (bf16[1024,384]{1,0:T(8,128)(2,1)S(1)}, bf16[1024,384]{1,0:T(8,128)(2,1)}, u32[]{:S(2)}) copy-start(bf16[1024,384]{1,0:T(8,128)(2,1)} %act.1) | copy-start | bytes 2359300
  1.8 1.1 %copy-start.1 = (bf16[1024,384]{1,0:T(8,128)(2,1)S(1)}, bf16[1024,384]{1,0:T(8,128)(2,1)}, u32[]{:S(2)}) copy-start(bf16[1024,384]{1,0:T(8,128)(2,1)} %cot.1) | copy-start | bytes 2359300
  2.9 1.0 %copy-start.2 = (bf16[576,384]{1,0:T(8,128)(2,1)S(1)}, bf16[576,384]{1,0:T(8,128)(2,1)}, u32[]{:S(2)}) copy-start(bf16[576,384]{1,0:T(8,128)(2,1)} %wts.1) | copy-start | bytes 1327108

commit v3 on v2

--- a/solution.py
+++ b/solution.py
@@ -79,14 +79,21 @@
     pl.semaphore_wait(barrier, greeted)
 
     w = wts.shape[0]
-    hw = w // 2
+    zs = 2 if Z % 2 == 0 and w % (4 * PAD) == 0 else 1
+    pw = w // (2 * zs)
+    h = z % zs
     partner = (y, z, x * CORES + other)
-
-    def half(shard, which):
-        return W.at[span((shard * 2 + which) * hw, hw)]
+    beside = (y, z + 1 - 2 * h, s)
+    across = (1 - y, z, s)
+
+    def piece_of(shard, group, which):
+        return W.at[span(shard * w + (group * zs + which) * pw, pw)]
 
     for j in range(1, X):
-        d = copy(("wx", j), wts.at[span(y * hw, hw)], half(s, y), (y, z, ((x + j) % X) * CORES + c))
+        d = copy(
+            ("wx", j), wts.at[span((y * zs + h) * pw, pw)], piece_of(s, y, h),
+            (y, z, ((x + j) % X) * CORES + c),
+        )
         d.start()
         pending.append(d)
     d = copy("wc", wts, W.at[span(s * w, w)], partner)
@@ -171,23 +178,34 @@
         def _():
             down.wait_recv()
 
-    forwards = []
+    def forward(name, ref, where):
+        d = copy(name, ref, ref, where)
+        d.start()
+        pending.append(d)
+
+    def arrived(name, ref):
+        copy(name, ref, ref, partner).wait_recv()
+
     for j in range(1, X):
         source = ((x + X - j) % X) * CORES + c
-        copy(("wx", j), half(source, y), half(source, y), partner).wait_recv()
-        d = copy(("wy", j), half(source, y), half(source, y), (1 - y, z, s))
-        d.start()
-        pending.append(d)
-        d = copy(("wca", j), half(source, y), half(source, y), partner)
-        d.start()
-        pending.append(d)
+        mine = piece_of(source, y, h)
+        arrived(("wx", j), mine)
+        if zs == 2:
+            forward(("wz", j), mine, beside)
+        forward(("wy", j, 0), mine, across)
+        forward(("wca", j, 0), mine, partner)
+    for j in range(1, X) if zs == 2 else ():
+        source = ((x + X - j) % X) * CORES + c
+        theirs = piece_of(source, y, 1 - h)
+        arrived(("wz", j), theirs)
+        forward(("wy", j, 1), theirs, across)
+        forward(("wca", j, 1), theirs, partner)
     for j in range(1, X):
         source = ((x + X - j) % X) * CORES + c
-        theirs = half(source, 1 - y)
-        copy(("wy", j), theirs, theirs, partner).wait_recv()
-        d = copy(("wcb", j), theirs, theirs, partner)
-        d.start()
-        pending.append(d)
+        for i in range(zs):
+            theirs = piece_of(source, 1 - y, (h + i) % zs)
+            arrived(("wy", j, i), theirs)
+            forward(("wcb", j, i), theirs, partner)
 
     for p in range(CHUNKS):
         local["a", p].wait()
@@ -200,8 +218,9 @@
     pending[X - 1].wait_recv()
     for j in range(1, X):
         source = ((x + X - j) % X) * CORES + other
-        copy(("wca", j), half(source, y), half(source, y), partner).wait_recv()
-        copy(("wcb", j), half(source, 1 - y), half(source, 1 - y), partner).wait_recv()
+        for i in range(zs):
+            arrived(("wca", j, i), piece_of(source, y, (h + i) % zs))
+            arrived(("wcb", j, i), piece_of(source, 1 - y, (h + i) % zs))
 
     def three(buf, p, width, start, back):
         taps = [buf[p, span(start + k * width * mp, tile), :] for k in range(3)]
@@ -246,16 +265,15 @@
         halo_send("hd", D2, 2, p)
 
     def grads(layer, buf, width, delta):
+        right = jnp.concatenate(
+            [delta[p, width * mp : width * mp + rows, :] for p in range(CHUNKS)], 0
+        )
         for k in range(3):
-            total = None
-            for p in range(CHUNKS):
-                part = lax.dot_general(
-                    buf[p, k * width * mp : k * width * mp + rows, :],
-                    delta[p, width * mp : width * mp + rows, :],
-                    (((0,), (0,)), ((), ())), preferred_element_type=f32,
-                )
-                total = part if total is None else total + part
-            G[layer, k * C : (k + 1) * C, :] = total
+            start = k * width * mp
+            left = jnp.concatenate([buf[p, start : start + rows, :] for p in range(CHUNKS)], 0)
+            G[layer, k * C : (k + 1) * C, :] = lax.dot_general(
+                left, right, (((0,), (0,)), ((), ())), preferred_element_type=f32
+            )
 
     hk = K // 2
     qk = hk // 2
@@ -361,15 +379,7 @@
         tiles(back_two)
         halo_send("he", D1, 1, p)
 
-    if fused:
-        cross_two = across_x(1, pair_two)
-    grads(0, A, 1, D1)
-    if fused:
-        pair_one = pair_send(0)
-        found_two = scatter(1, cross_two)
-        cross_one = across_x(0, pair_one)
-
-    for p in range(CHUNKS):
+    def finish(p):
         halo_wait("he", D1, 1, p)
 
         def back_one(start):
@@ -379,8 +389,6 @@
             ).astype(bf16)
 
         tiles(back_one)
-        if fused and p == 0:
-            found_one = scatter(0, cross_one)
         for j in range(1, S):
             to = (s + j) % S
             d = copy(
@@ -392,9 +400,21 @@
         out[span(s * m + p * mp, mp), :] = OG[p, span(s * mp, mp), :]
 
     if fused:
+        cross_two = across_x(1, pair_two)
+    for p in range(CHUNKS // 2):
+        finish(p)
+    grads(0, A, 1, D1)
+    if fused:
+        pair_one = pair_send(0)
+        found_two = scatter(1, cross_two)
+        cross_one = across_x(0, pair_one)
+    for p in range(CHUNKS // 2, CHUNKS):
+        finish(p)
+    if fused:
         gather(1, found_two)
+        found_one = scatter(0, cross_one)
+        pass_on(1)
         gather(0, found_one)
-        pass_on(1)
         pass_on(0)
         collect(1)
         collect(0)
@@ -427,7 +447,7 @@
     qk = K // 4 if fused else PAD
     hk = K // 2 if fused else PAD
     bf16, f32 = jnp.bfloat16, jnp.float32
-    semaphores = (S - 1) * CHUNKS * 3 + 8 * CHUNKS + 1 + 4 * X + 2 * (2 + Z) + 1 + 2 * Z + 8
+    semaphores = (S - 1) * CHUNKS * 3 + 8 * CHUNKS + 1 + 8 * X + 2 * (2 + Z) + 1 + 2 * Z + 8
     vmem = pl.BlockSpec(memory_space=pltpu.VMEM)
     input_grad, grads = pl.pallas_call(
         functools.partial(kernel, groups, Z, S, fused),
@@ -462,7 +482,7 @@
             pltpu.SemaphoreType.DMA((2 * CHUNKS + 1,)),
         ],
         compiler_params=pltpu.CompilerParams(
-            collective_id=0, has_side_effects=True, vmem_limit_bytes=48 * 1024 * 1024
+            collective_id=0, has_side_effects=True, vmem_limit_bytes=62 * 1024 * 1024
         ),
         name="layers_backward",
     )(activations, cotangent, weights)

time: 77.7 us -> 82.7 us (1.064)
  Pallas kernels: 71.7 us -> 78.8 us
  local copies, waits for them, and re-layouts: 5.06 us -> 3.09 us
    pallas_call x1, Pallas kernels: 71.7 us -> 78.8 us  [per_device(): pl.pallas_call(functools.partial(kernel, groups, Z, S, fused), out_shape=...]
    unnamed x8 -> x4, local copies, waits for them, and re-layouts: 5.06 us -> 3.09 us
where the time goes in v3:
time: 82.7 us; the launch traced here: 82.6 us
  Pallas kernels  78.8 us (95%)
  local copies, waits for them, and re-layouts  3.09 us (4%)
    pallas_call x1, Pallas kernels, per_device(): pl.pallas_call(functools.partial(kernel, groups, Z, S, fused), out_shape=...  78.8 us
    unnamed x4, local copies, waits for them, and re-layouts  3.09 us

profile of v3, /device:TPU:0, one launch (start us, length us, event | category | flops | bytes accessed | tf_op | source)
XLA Modules:
  0.0 82.6 jit_solution(10863115395801839361)
XLA Ops:
  0.6 78.8 %layers_backward.1 = (bf16[1024,384]{1,0:T(8,128)(2,1)}, f32[576,384]{1,0:T(8,128)}) custom-call(bf16[1024,384]{1,0:T(8,128)(2,1)} %act.1, bf16[1024,384]{1,0:T(8,128)(2,1)} %cot.1, bf16[576,384]{1,0:T(8,128)(2,1)} %wts.1), custom_call_target="tpu_custom_call" | custom-call | tf_op jit(solution)/shard_map/layers_backward/pallas_call | solution.py:452
  79.5 0.0 copy-start
  79.5 2.2 %copy.7 = bf16[1024,384]{1,0:T(8,128)(2,1)} copy(bf16[1024,384]{1,0:T(8,128)(2,1)} %get-tuple-element.4) | data formatting | bytes 1572864
  81.6 0.0 copy-done
  81.6 0.9 %copy.8 = f32[576,384]{1,0:T(8,128)} copy(f32[576,384]{1,0:T(8,128)S(1)} %copy-done) | data formatting | bytes 1769472
Async XLA Ops:
  79.5 2.2 %copy-start = (f32[576,384]{1,0:T(8,128)S(1)}, f32[576,384]{1,0:T(8,128)}, u32[]{:S(2)}) copy-start(f32[576,384]{1,0:T(8,128)} %get-tuple-element.5) | copy-start | bytes 2654212

commit v4 on v3

--- a/solution.py
+++ b/solution.py
@@ -117,7 +117,7 @@
         )
         return found
 
-    acts = [spread("a", act, A, 1, p) for p in range(CHUNKS)]
+    acts = [spread("a", act, A, 1, 0)]
     bring("w", wts, W.at[span(s * w, w)])
 
     def edges(buf, width):
@@ -194,12 +194,23 @@
             forward(("wz", j), mine, beside)
         forward(("wy", j, 0), mine, across)
         forward(("wca", j, 0), mine, partner)
+    acts += [spread("a", act, A, 1, p) for p in range(1, CHUNKS)]
+
+    def edges_out(p):
+        local["a", p].wait()
+        for d in acts[p]:
+            d.wait_recv()
+        halo_send("ha", A, 1, p)
+
+    edges_out(0)
     for j in range(1, X) if zs == 2 else ():
         source = ((x + X - j) % X) * CORES + c
         theirs = piece_of(source, y, 1 - h)
         arrived(("wz", j), theirs)
         forward(("wy", j, 1), theirs, across)
         forward(("wca", j, 1), theirs, partner)
+    for p in range(1, CHUNKS):
+        edges_out(p)
     for j in range(1, X):
         source = ((x + X - j) % X) * CORES + c
         for i in range(zs):
@@ -207,11 +218,6 @@
             arrived(("wy", j, i), theirs)
             forward(("wcb", j, i), theirs, partner)
 
-    for p in range(CHUNKS):
-        local["a", p].wait()
-        for d in acts[p]:
-            d.wait_recv()
-        halo_send("ha", A, 1, p)
     cots = [spread("c", cot, CT, 0, p) for p in range(CHUNKS)]
 
     local["w"].wait()
@@ -389,6 +395,8 @@
             ).astype(bf16)
 
         tiles(back_one)
+
+    def give_out(p):
         for j in range(1, S):
             to = (s + j) % S
             d = copy(
@@ -401,20 +409,23 @@
 
     if fused:
         cross_two = across_x(1, pair_two)
-    for p in range(CHUNKS // 2):
-        finish(p)
     grads(0, A, 1, D1)
     if fused:
         pair_one = pair_send(0)
         found_two = scatter(1, cross_two)
         cross_one = across_x(0, pair_one)
-    for p in range(CHUNKS // 2, CHUNKS):
+    finish(0)
+    if fused:
+        found_one = scatter(0, cross_one)
+    give_out(0)
+    if fused:
+        gather(1, found_two)
+    for p in range(1, CHUNKS):
         finish(p)
-    if fused:
-        gather(1, found_two)
-        found_one = scatter(0, cross_one)
+        give_out(p)
+    if fused:
+        gather(0, found_one)
         pass_on(1)
-        gather(0, found_one)
         pass_on(0)
         collect(1)
         collect(0)
@@ -482,7 +493,7 @@
             pltpu.SemaphoreType.DMA((2 * CHUNKS + 1,)),
         ],
         compiler_params=pltpu.CompilerParams(
-            collective_id=0, has_side_effects=True, vmem_limit_bytes=62 * 1024 * 1024
+            collective_id=0, has_side_effects=True, vmem_limit_bytes=48 * 1024 * 1024
         ),
         name="layers_backward",
     )(activations, cotangent, weights)

time: 82.7 us -> 78.3 us (0.947)
  Pallas kernels: 78.8 us -> 72.4 us
  local copies, waits for them, and re-layouts: 3.09 us -> 5.06 us
    pallas_call x1, Pallas kernels: 78.8 us -> 72.4 us  [per_device(): pl.pallas_call(functools.partial(kernel, groups, Z, S, fused), out_shape=...]
    unnamed x4 -> x8, local copies, waits for them, and re-layouts: 3.09 us -> 5.06 us
where the time goes in v4:
time: 78.3 us; the launch traced here: 78.1 us
  Pallas kernels  72.4 us (92%)
  local copies, waits for them, and re-layouts  5.06 us (6%)
    pallas_call x1, Pallas kernels, per_device(): pl.pallas_call(functools.partial(kernel, groups, Z, S, fused), out_shape=...  72.4 us
    unnamed x8, local copies, waits for them, and re-layouts  5.06 us

profile of v4, /device:TPU:0, one launch (start us, length us, event | category | flops | bytes accessed | tf_op | source)
XLA Modules:
  0.0 78.1 jit_solution(15555496627097077890)
XLA Ops:
  0.6 0.0 copy-start
  0.6 1.1 %copy-done = bf16[1024,384]{1,0:T(8,128)(2,1)S(1)} copy-done((bf16[1024,384]{1,0:T(8,128)(2,1)S(1)}, bf16[1024,384]{1,0:T(8,128)(2,1)}, u32[]{:S(2)}) %copy-start) | copy-done | bytes 786456
  1.8 0.0 copy-start.1
  1.8 1.1 %copy-done.1 = bf16[1024,384]{1,0:T(8,128)(2,1)S(1)} copy-done((bf16[1024,384]{1,0:T(8,128)(2,1)S(1)}, bf16[1024,384]{1,0:T(8,128)(2,1)}, u32[]{:S(2)}) %copy-start.1) | copy-done | bytes 786456
  2.9 0.0 copy-start.2
  2.9 1.0 %copy-done.2 = bf16[576,384]{1,0:T(8,128)(2,1)S(1)} copy-done((bf16[576,384]{1,0:T(8,128)(2,1)S(1)}, bf16[576,384]{1,0:T(8,128)(2,1)}, u32[]{:S(2)}) %copy-start.2) | copy-done | bytes 442392
  3.9 72.4 %layers_backward.1 = (bf16[1024,384]{1,0:T(8,128)(2,1)S(1)}, f32[576,384]{1,0:T(8,128)S(1)}) custom-call(bf16[1024,384]{1,0:T(8,128)(2,1)S(1)} %copy-done, bf16[1024,384]{1,0:T(8,128)(2,1)S(1)} %copy-done.1, bf16[576,384]{1,0:T(8,128)(2,1)S(1)} %copy-done.2), custom_call_target="tpu_custom_call" | custom-call | tf_op jit(solution)/shard_map/layers_backward/pallas_call | solution.py:463
  76.3 0.9 %copy.7 = bf16[1024,384]{1,0:T(8,128)(2,1)} copy(bf16[1024,384]{1,0:T(8,128)(2,1)S(1)} %get-tuple-element.4) | data formatting | bytes 1572864
  77.2 0.9 %copy.8 = f32[576,384]{1,0:T(8,128)} copy(f32[576,384]{1,0:T(8,128)S(1)} %get-tuple-element.5) | data formatting | bytes 1769472
Async XLA Ops:
  0.6 1.1 %copy-start = (bf16[1024,384]{1,0:T(8,128)(2,1)S(1)}, bf16[1024,384]{1,0:T(8,128)(2,1)}, u32[]{:S(2)}) copy-start(bf16[1024,384]{1,0:T(8,128)(2,1)} %act.1) | copy-start | bytes 2359300
  1.8 1.1 %copy-start.1 = (bf16[1024,384]{1,0:T(8,128)(2,1)S(1)}, bf16[1024,384]{1,0:T(8,128)(2,1)}, u32[]{:S(2)}) copy-start(bf16[1024,384]{1,0:T(8,128)(2,1)} %cot.1) | copy-start | bytes 2359300
  2.9 1.0 %copy-start.2 = (bf16[576,384]{1,0:T(8,128)(2,1)S(1)}, bf16[576,384]{1,0:T(8,128)(2,1)}, u32[]{:S(2)}) copy-start(bf16[576,384]{1,0:T(8,128)(2,1)} %wts.1) | copy-start | bytes 1327108

commit v5 on v2

--- a/solution.py
+++ b/solution.py
@@ -381,6 +381,8 @@
         tiles(back_one)
         if fused and p == 0:
             found_one = scatter(0, cross_one)
+        if fused and p == CHUNKS - 1:
+            gather(1, found_two)
         for j in range(1, S):
             to = (s + j) % S
             d = copy(
@@ -392,9 +394,8 @@
         out[span(s * m + p * mp, mp), :] = OG[p, span(s * mp, mp), :]
 
     if fused:
-        gather(1, found_two)
+        pass_on(1)
         gather(0, found_one)
-        pass_on(1)
         pass_on(0)
         collect(1)
         collect(0)

time: 77.7 us -> 79.1 us (1.018)
  Pallas kernels: 71.7 us -> 73.2 us
    pallas_call x1, Pallas kernels: 71.7 us -> 73.2 us  [per_device(): pl.pallas_call(functools.partial(kernel, groups, Z, S, fused), out_shape=...]
where the time goes in v5:
time: 79.1 us; the launch traced here: 78.9 us
  Pallas kernels  73.2 us (93%)
  local copies, waits for them, and re-layouts  5.06 us (6%)
    pallas_call x1, Pallas kernels, per_device(): pl.pallas_call(functools.partial(kernel, groups, Z, S, fused), out_shape=...  73.2 us
    unnamed x8, local copies, waits for them, and re-layouts  5.06 us

profile of v5, /device:TPU:0, one launch (start us, length us, event | category | flops | bytes accessed | tf_op | source)
XLA Modules:
  0.0 78.9 jit_solution(14360218010784470071)
XLA Ops:
  0.6 0.0 copy-start
  0.6 1.1 %copy-done = bf16[1024,384]{1,0:T(8,128)(2,1)S(1)} copy-done((bf16[1024,384]{1,0:T(8,128)(2,1)S(1)}, bf16[1024,384]{1,0:T(8,128)(2,1)}, u32[]{:S(2)}) %copy-start) | copy-done | bytes 786456
  1.8 0.0 copy-start.1
  1.8 1.1 %copy-done.1 = bf16[1024,384]{1,0:T(8,128)(2,1)S(1)} copy-done((bf16[1024,384]{1,0:T(8,128)(2,1)S(1)}, bf16[1024,384]{1,0:T(8,128)(2,1)}, u32[]{:S(2)}) %copy-start.1) | copy-done | bytes 786456
  2.9 0.0 copy-start.2
  2.9 1.0 %copy-done.2 = bf16[576,384]{1,0:T(8,128)(2,1)S(1)} copy-done((bf16[576,384]{1,0:T(8,128)(2,1)S(1)}, bf16[576,384]{1,0:T(8,128)(2,1)}, u32[]{:S(2)}) %copy-start.2) | copy-done | bytes 442392
  3.9 73.2 %layers_backward.1 = (bf16[1024,384]{1,0:T(8,128)(2,1)S(1)}, f32[576,384]{1,0:T(8,128)S(1)}) custom-call(bf16[1024,384]{1,0:T(8,128)(2,1)S(1)} %copy-done, bf16[1024,384]{1,0:T(8,128)(2,1)S(1)} %copy-done.1, bf16[576,384]{1,0:T(8,128)(2,1)S(1)} %copy-done.2), custom_call_target="tpu_custom_call" | custom-call | tf_op jit(solution)/shard_map/layers_backward/pallas_call | solution.py:433
  77.1 0.9 %copy.7 = bf16[1024,384]{1,0:T(8,128)(2,1)} copy(bf16[1024,384]{1,0:T(8,128)(2,1)S(1)} %get-tuple-element.4) | data formatting | bytes 1572864
  78.0 0.9 %copy.8 = f32[576,384]{1,0:T(8,128)} copy(f32[576,384]{1,0:T(8,128)S(1)} %get-tuple-element.5) | data formatting | bytes 1769472
Async XLA Ops:
  0.6 1.1 %copy-start = (bf16[1024,384]{1,0:T(8,128)(2,1)S(1)}, bf16[1024,384]{1,0:T(8,128)(2,1)}, u32[]{:S(2)}) copy-start(bf16[1024,384]{1,0:T(8,128)(2,1)} %act.1) | copy-start | bytes 2359300
  1.8 1.1 %copy-start.1 = (bf16[1024,384]{1,0:T(8,128)(2,1)S(1)}, bf16[1024,384]{1,0:T(8,128)(2,1)}, u32[]{:S(2)}) copy-start(bf16[1024,384]{1,0:T(8,128)(2,1)} %cot.1) | copy-start | bytes 2359300
  2.9 1.0 %copy-start.2 = (bf16[576,384]{1,0:T(8,128)(2,1)S(1)}, bf16[576,384]{1,0:T(8,128)(2,1)}, u32[]{:S(2)}) copy-start(bf16[576,384]{1,0:T(8,128)(2,1)} %wts.1) | copy-start | bytes 1327108
